TPU v7x, 32 devices: a whole 2x2x4 slice. The times are simulated.
32 devices in a mesh: groups: 2 (over y), ctx: 4 (over z), head: 2 (over x), rep: 2 (over core).
Axes of the slice: x: 2, y: 2, z: 4, core: 2. Of those that a mesh axis runs over, the one named last changes fastest.
Arguments:
- queries: bfloat16 [4096, 4096], P(('groups', 'ctx', 'rep'), 'head'), parts along dimension 0, may hold values from -20 to 20
- keys: bfloat16 [4096, 512], P(('groups', 'ctx', 'rep'), 'head'), parts along dimension 0, may hold values from -20 to 20
- values: bfloat16 [4096, 512], P(('groups', 'ctx', 'rep'), 'head'), parts along dimension 0, may hold values from -6 to 6
- span_order: int32 [16], P('groups'), parts along dimension 0, may hold values from 0 to 7, each once
Outputs:
- attended: bfloat16 [4096, 4096], P(('groups', 'ctx', 'rep'), 'head'), parts along dimension 0
- heavy: float32 [8, 2048], P(('groups', 'head'), ('ctx', 'rep')), parts along dimension 0
There are 2 independent parts, one for each index of `groups`. A program takes and returns all parts, laid end to end along the dimension named above; each array names one. Nothing has to cross between parts.
Inputs may be any that keep to these rules, and one draw needn't show every extreme that they name: `span_order`: every sub-block of 256 positions stands in exactly one slot.
All inputs are finite; a program needn't handle non-finite values.
Results may differ from a plain program's by a relative error of at most 0.0045.
Values may be sent and summed in bfloat16 or wider, within the bound.
A program may use at most 64 MiB of HBM per device.

v0:
```python
import jax
import jax.numpy as jnp
from jax import lax
from jax.sharding import PartitionSpec as P

HEAD_WIDTH = 128
SPLIT = 1


NEG = -1e30


def positions(order_table, first_row, count, sub_rows):
    row_index = first_row + jnp.arange(count, dtype=jnp.int32)
    return jnp.take(order_table, row_index // sub_rows) * sub_rows + row_index % sub_rows


def absorb(carried, key_block, value_block, key_pos, query_part, pos_part, score_scale):
    maxima, totals, sums = carried
    scores = (
        jnp.einsum("qhgd,khd->hgqk", query_part, key_block, preferred_element_type=jnp.float32)
        * score_scale
    )
    allowed = key_pos[None, None, None, :] <= pos_part[None, None, :, None]
    scores = jnp.where(allowed, scores, NEG)
    fresh = jnp.maximum(maxima, jnp.max(scores, axis=-1))
    expo = jnp.where(allowed, jnp.exp(scores - fresh[..., None]), 0.0)
    factor = jnp.exp(maxima - fresh)
    totals = totals * factor + jnp.sum(expo, axis=-1)
    weights = expo.astype(jnp.bfloat16)
    sums = sums * factor[..., None] + jnp.einsum(
        "hgqk,khd->hgqd", weights, value_block, preferred_element_type=jnp.float32
    )
    return (fresh, totals, sums)


def on_device(queries, keys, values, span_order):
    row_count = queries.shape[0]
    kv_heads = keys.shape[1] // HEAD_WIDTH
    group_width = queries.shape[1] // keys.shape[1]
    sub_rows = row_count // SPLIT
    score_scale = HEAD_WIDTH ** (-0.5)
    device_rank = lax.axis_index(("ctx", "rep"))
    query_pos = positions(span_order, device_rank * row_count, row_count, sub_rows)
    query_mat = queries.reshape(row_count, kv_heads, group_width, HEAD_WIDTH)

    def visit(carried, key_block, value_block, key_pos):
        needed = jnp.min(key_pos) <= jnp.max(query_pos)
        return lax.cond(
            needed,
            lambda inner: absorb(
                inner, key_block, value_block, key_pos, query_mat, query_pos, score_scale
            ),
            lambda inner: inner,
            carried,
        )

    initial = (
        jnp.full((kv_heads, group_width, row_count), NEG, jnp.float32),
        jnp.zeros((kv_heads, group_width, row_count), jnp.float32),
        jnp.zeros((kv_heads, group_width, row_count, HEAD_WIDTH), jnp.float32),
    )
    carried = initial
    key_piece = lax.all_gather(keys, ("ctx", "rep"), axis=0, tiled=True)
    value_piece = lax.all_gather(values, ("ctx", "rep"), axis=0, tiled=True)
    length = key_piece.shape[0]
    count = length // row_count
    key_blocks = key_piece.reshape(count, row_count, kv_heads, HEAD_WIDTH)
    value_blocks = value_piece.reshape(count, row_count, kv_heads, HEAD_WIDTH)
    starts = row_count * jnp.arange(count, dtype=jnp.int32)

    def advance(inner, item):
        key_block, value_block, block_start = item
        key_pos = positions(span_order, block_start, row_count, sub_rows)
        return (visit(inner, key_block, value_block, key_pos), None)

    carried, unused = lax.scan(advance, carried, (key_blocks, value_blocks, starts))
    maxima, totals, sums = carried

    def column_block(key_block, key_pos):

        def compute():
            scores = (
                jnp.einsum(
                    "qhgd,khd->hgqk", query_mat, key_block, preferred_element_type=jnp.float32
                )
                * score_scale
            )
            allowed = key_pos[None, None, None, :] <= query_pos[None, None, :, None]
            expo = jnp.where(
                allowed, jnp.exp(jnp.where(allowed, scores, NEG) - maxima[..., None]), 0.0
            )
            return jnp.sum(expo / totals[..., None], axis=(1, 2))

        needed = jnp.min(key_pos) <= jnp.max(query_pos)
        return lax.cond(
            needed, compute, lambda: jnp.zeros((kv_heads, key_block.shape[0]), jnp.float32)
        )

    key_piece = lax.all_gather(keys, ("ctx", "rep"), axis=0, tiled=True)
    length = key_piece.shape[0]
    count = length // row_count
    key_blocks = key_piece.reshape(count, row_count, kv_heads, HEAD_WIDTH)
    starts = row_count * jnp.arange(count, dtype=jnp.int32)

    def single_block(item):
        key_block, block_start = item
        return column_block(key_block, positions(span_order, block_start, row_count, sub_rows))

    column_span = lax.map(single_block, (key_blocks, starts))
    column_terms = column_span.transpose(1, 0, 2).reshape(kv_heads, length)
    heavy = (
        lax.psum_scatter(column_terms, ("ctx", "rep"), scatter_dimension=1, tiled=True)
        / group_width
    )
    attended = (
        (sums / totals[..., None])
        .transpose(2, 0, 1, 3)
        .reshape(row_count, kv_heads * group_width * HEAD_WIDTH)
        .astype(jnp.bfloat16)
    )
    return (attended, heavy)


def solution(mesh):
    placed = (
        P(("groups", "ctx", "rep"), "head"),
        P(("groups", "ctx", "rep"), "head"),
        P(("groups", "ctx", "rep"), "head"),
        P("groups"),
    )
    return jax.shard_map(
        on_device,
        mesh=mesh,
        in_specs=placed,
        out_specs=(P(("groups", "ctx", "rep"), "head"), P(("groups", "head"), ("ctx", "rep"))),
        check_vma=False,
    )
```

profile of v0, /device:TPU:0, one launch (start us, length us, event | category | flops | bytes accessed | tf_op | source)
XLA Modules:
  0.0 314.1 jit_solution(13477664170074422514)
XLA Ops:
  11.6 5.8 %fusion.41 = (s32[]{:T(128)}, s32[256]{0:T(256)S(1)}) fusion(s32[]{:T(128)} %bitcast.37, s32[]{:T(128)} %bitcast.36, s32[]{:T(128)} %bitcast.35, s32[]{:T(128)} %bitcast.34, s32[]{:T(128)} %bitcast.33, s32[]{:T(128)} %bitcast.32, s32[]{:T(128)} %bitcast.31, s32[]{:T(128)} %bitcast.30, s32[]{:T(128)S(6)} %mul.61), kind=kLoop, calls=%fused_computation.91 | loop fusion | flops 11263 | bytes 1064 | tf_op jit(solution)/shard_map/while/body/eval_jaxpr/reduce_max | solution.py:48
  17.4 16.8 %all-gather.3.cloned.1.call-done = bf16[2048,256]{1,0:T(8,128)(2,1)} async-done(((bf16[256,256]{1,0:T(8,128)(2,1)}), bf16[2048,256]{1,0:T(8,128)(2,1)}) %all-gather.3.cloned.1.call-update) | async-done | bytes 1048592 | tf_op jit(solution)/shard_map/all_gather | solution.py:64
  36.8 21.0 %all-gather.5.cloned.1.call-done = bf16[2048,256]{1,0:T(8,128)(2,1)} async-done(((bf16[256,256]{1,0:T(8,128)(2,1)}), bf16[2048,256]{1,0:T(8,128)(2,1)}) %all-gather.5.cloned.1.call-update) | async-done | bytes 1048592 | tf_op jit(solution)/shard_map/all_gather | solution.py:65
  60.5 88.4 %while.28 = (s32[]{:T(128)}, f32[2,8,256]{2,1,0:T(8,128)S(1)}, f32[2,8,256]{2,1,0:T(8,128)S(1)}, f32[2,8,256,128]{3,2,1,0:T(8,128)S(1)}, s32[8]{0:T(128)S(1)}, /...) while((s32[]{:T(128)}, f32[2,8,256]{2,1,0:T(8,128)S(1)}, ...), condition=%wide.region_7.9_spmd, body=%wide.region_1.8_spmd.sunk | while | flops 551635968 | bytes 18616696 | solution.py:77
  61.9 6.3 %fusion.53 = (s32[]{:T(128)}, s32[256]{0:T(256)S(1)}) fusion(s32[]{:T(128)} %bitcast.105, s32[]{:T(128)} %bitcast.106, s32[]{:T(128)} %bitcast.107, s32[]{:T(128)} %bitcast.108, s32[]{:T(128)} %bitcast.109, s32[]{:T(128)} %bitcast.110, s32[]{:T(128)} %bitcast.111, s32[]{:T(128)} %bitcast.112, s32[]{:T(128)} %bitcast.113), kind=kLoop, calls=%fused_computation.89.clone.1 | loop fusion | flops 11263 | bytes 1064 | tf_op jit(solution)/shard_map/while/body/eval_jaxpr/reduce_min | solution.py:48
  69.4 5.9 %conditional.4 = ((f32[2,8,256]{2,1,0:T(8,128)S(1)}, f32[2,8,256]{2,1,0:T(8,128)S(1)}, f32[2,8,256,128]{3,2,1,0:T(8,128)S(1)})) conditional(s32[]{:T(128)} %convert_element_type.38, (f32[2,8,256]{2,1,0:T(8,128)S(1)}, f32[2,8,256]{2,1,0:T(8,128)S(1)}, f32[2,8,256,128]{3,2,1,0:T(8,128)S(1)}) %tuple.114, (s32[256]{0:T(256)S(1)}, s32[256]{0:T(256)S(1)}, ...), branch_computations={%region_3.4_spmd, %region_4.7_spmd} | conditional | flops 551624704 | bytes 18615328 | solution.py:49
  72.2 3.0 multiply_add_fusion
  76.6 6.3 %fusion.53 = (s32[]{:T(128)}, s32[256]{0:T(256)S(1)}) fusion(s32[]{:T(128)} %bitcast.105, s32[]{:T(128)} %bitcast.106, s32[]{:T(128)} %bitcast.107, s32[]{:T(128)} %bitcast.108, s32[]{:T(128)} %bitcast.109, s32[]{:T(128)} %bitcast.110, s32[]{:T(128)} %bitcast.111, s32[]{:T(128)} %bitcast.112, s32[]{:T(128)} %bitcast.113), kind=kLoop, calls=%fused_computation.89.clone.1 | loop fusion | flops 11263 | bytes 1064 | tf_op jit(solution)/shard_map/while/body/eval_jaxpr/reduce_min | solution.py:48
  85.4 6.3 %fusion.53 = (s32[]{:T(128)}, s32[256]{0:T(256)S(1)}) fusion(s32[]{:T(128)} %bitcast.105, s32[]{:T(128)} %bitcast.106, s32[]{:T(128)} %bitcast.107, s32[]{:T(128)} %bitcast.108, s32[]{:T(128)} %bitcast.109, s32[]{:T(128)} %bitcast.110, s32[]{:T(128)} %bitcast.111, s32[]{:T(128)} %bitcast.112, s32[]{:T(128)} %bitcast.113), kind=kLoop, calls=%fused_computation.89.clone.1 | loop fusion | flops 11263 | bytes 1064 | tf_op jit(solution)/shard_map/while/body/eval_jaxpr/reduce_min | solution.py:48
  94.3 6.3 %fusion.53 = (s32[]{:T(128)}, s32[256]{0:T(256)S(1)}) fusion(s32[]{:T(128)} %bitcast.105, s32[]{:T(128)} %bitcast.106, s32[]{:T(128)} %bitcast.107, s32[]{:T(128)} %bitcast.108, s32[]{:T(128)} %bitcast.109, s32[]{:T(128)} %bitcast.110, s32[]{:T(128)} %bitcast.111, s32[]{:T(128)} %bitcast.112, s32[]{:T(128)} %bitcast.113), kind=kLoop, calls=%fused_computation.89.clone.1 | loop fusion | flops 11263 | bytes 1064 | tf_op jit(solution)/shard_map/while/body/eval_jaxpr/reduce_min | solution.py:48
  101.8 5.9 %conditional.4 = ((f32[2,8,256]{2,1,0:T(8,128)S(1)}, f32[2,8,256]{2,1,0:T(8,128)S(1)}, f32[2,8,256,128]{3,2,1,0:T(8,128)S(1)})) conditional(s32[]{:T(128)} %convert_element_type.38, (f32[2,8,256]{2,1,0:T(8,128)S(1)}, f32[2,8,256]{2,1,0:T(8,128)S(1)}, f32[2,8,256,128]{3,2,1,0:T(8,128)S(1)}) %tuple.114, (s32[256]{0:T(256)S(1)}, s32[256]{0:T(256)S(1)}, ...), branch_computations={%region_3.4_spmd, %region_4.7_spmd} | conditional | flops 551624704 | bytes 18615328 | solution.py:49
  104.7 3.0 multiply_add_fusion
  109.0 6.3 %fusion.53 = (s32[]{:T(128)}, s32[256]{0:T(256)S(1)}) fusion(s32[]{:T(128)} %bitcast.105, s32[]{:T(128)} %bitcast.106, s32[]{:T(128)} %bitcast.107, s32[]{:T(128)} %bitcast.108, s32[]{:T(128)} %bitcast.109, s32[]{:T(128)} %bitcast.110, s32[]{:T(128)} %bitcast.111, s32[]{:T(128)} %bitcast.112, s32[]{:T(128)} %bitcast.113), kind=kLoop, calls=%fused_computation.89.clone.1 | loop fusion | flops 11263 | bytes 1064 | tf_op jit(solution)/shard_map/while/body/eval_jaxpr/reduce_min | solution.py:48
  117.9 6.3 %fusion.53 = (s32[]{:T(128)}, s32[256]{0:T(256)S(1)}) fusion(s32[]{:T(128)} %bitcast.105, s32[]{:T(128)} %bitcast.106, s32[]{:T(128)} %bitcast.107, s32[]{:T(128)} %bitcast.108, s32[]{:T(128)} %bitcast.109, s32[]{:T(128)} %bitcast.110, s32[]{:T(128)} %bitcast.111, s32[]{:T(128)} %bitcast.112, s32[]{:T(128)} %bitcast.113), kind=kLoop, calls=%fused_computation.89.clone.1 | loop fusion | flops 11263 | bytes 1064 | tf_op jit(solution)/shard_map/while/body/eval_jaxpr/reduce_min | solution.py:48
  125.3 5.9 %conditional.4 = ((f32[2,8,256]{2,1,0:T(8,128)S(1)}, f32[2,8,256]{2,1,0:T(8,128)S(1)}, f32[2,8,256,128]{3,2,1,0:T(8,128)S(1)})) conditional(s32[]{:T(128)} %convert_element_type.38, (f32[2,8,256]{2,1,0:T(8,128)S(1)}, f32[2,8,256]{2,1,0:T(8,128)S(1)}, f32[2,8,256,128]{3,2,1,0:T(8,128)S(1)}) %tuple.114, (s32[256]{0:T(256)S(1)}, s32[256]{0:T(256)S(1)}, ...), branch_computations={%region_3.4_spmd, %region_4.7_spmd} | conditional | flops 551624704 | bytes 18615328 | solution.py:49
  128.2 3.0 multiply_add_fusion
  132.6 6.3 %fusion.53 = (s32[]{:T(128)}, s32[256]{0:T(256)S(1)}) fusion(s32[]{:T(128)} %bitcast.105, s32[]{:T(128)} %bitcast.106, s32[]{:T(128)} %bitcast.107, s32[]{:T(128)} %bitcast.108, s32[]{:T(128)} %bitcast.109, s32[]{:T(128)} %bitcast.110, s32[]{:T(128)} %bitcast.111, s32[]{:T(128)} %bitcast.112, s32[]{:T(128)} %bitcast.113), kind=kLoop, calls=%fused_computation.89.clone.1 | loop fusion | flops 11263 | bytes 1064 | tf_op jit(solution)/shard_map/while/body/eval_jaxpr/reduce_min | solution.py:48
  141.4 6.3 %fusion.53 = (s32[]{:T(128)}, s32[256]{0:T(256)S(1)}) fusion(s32[]{:T(128)} %bitcast.105, s32[]{:T(128)} %bitcast.106, s32[]{:T(128)} %bitcast.107, s32[]{:T(128)} %bitcast.108, s32[]{:T(128)} %bitcast.109, s32[]{:T(128)} %bitcast.110, s32[]{:T(128)} %bitcast.111, s32[]{:T(128)} %bitcast.112, s32[]{:T(128)} %bitcast.113), kind=kLoop, calls=%fused_computation.89.clone.1 | loop fusion | flops 11263 | bytes 1064 | tf_op jit(solution)/shard_map/while/body/eval_jaxpr/reduce_min | solution.py:48
  148.9 79.5 %while.29 = (s32[]{:T(128)}, f32[8,2,256]{2,1,0:T(2,128)S(1)}, s32[8]{0:T(128)S(1)}, s32[8]{0:T(128)S(1)}, s32[]{:T(128)}, /*index=5*/s32[256]{0:T(256)S(1)}, bf...) while((s32[]{:T(128)}, f32[8,2,256]{2,1,0:T(2,128)S(1)}, ...), condition=%wide.region_13.15_spmd, body=%wide.region_8.14_spmd.sunk | while | flops 274803200 | bytes 1353523 | solution.py:110
  150.2 6.3 %fusion.55 = (s32[]{:T(128)}, s32[256]{0:T(256)S(1)}) fusion(s32[]{:T(128)} %bitcast.114, s32[]{:T(128)} %bitcast.115, s32[]{:T(128)} %bitcast.116, s32[]{:T(128)} %bitcast.117, s32[]{:T(128)} %bitcast.118, s32[]{:T(128)} %bitcast.119, s32[]{:T(128)} %bitcast.120, s32[]{:T(128)} %bitcast.121, s32[]{:T(128)} %bitcast.122), kind=kLoop, calls=%fused_computation.90.clone.1 | loop fusion | flops 11263 | bytes 1064 | tf_op jit(solution)/shard_map/while/body/eval_jaxpr/reduce_min | solution.py:95
  157.7 3.0 conditional.5
  162.1 6.3 %fusion.55 = (s32[]{:T(128)}, s32[256]{0:T(256)S(1)}) fusion(s32[]{:T(128)} %bitcast.114, s32[]{:T(128)} %bitcast.115, s32[]{:T(128)} %bitcast.116, s32[]{:T(128)} %bitcast.117, s32[]{:T(128)} %bitcast.118, s32[]{:T(128)} %bitcast.119, s32[]{:T(128)} %bitcast.120, s32[]{:T(128)} %bitcast.121, s32[]{:T(128)} %bitcast.122), kind=kLoop, calls=%fused_computation.90.clone.1 | loop fusion | flops 11263 | bytes 1064 | tf_op jit(solution)/shard_map/while/body/eval_jaxpr/reduce_min | solution.py:95
  170.9 6.3 %fusion.55 = (s32[]{:T(128)}, s32[256]{0:T(256)S(1)}) fusion(s32[]{:T(128)} %bitcast.114, s32[]{:T(128)} %bitcast.115, s32[]{:T(128)} %bitcast.116, s32[]{:T(128)} %bitcast.117, s32[]{:T(128)} %bitcast.118, s32[]{:T(128)} %bitcast.119, s32[]{:T(128)} %bitcast.120, s32[]{:T(128)} %bitcast.121, s32[]{:T(128)} %bitcast.122), kind=kLoop, calls=%fused_computation.90.clone.1 | loop fusion | flops 11263 | bytes 1064 | tf_op jit(solution)/shard_map/while/body/eval_jaxpr/reduce_min | solution.py:95
  179.7 6.3 %fusion.55 = (s32[]{:T(128)}, s32[256]{0:T(256)S(1)}) fusion(s32[]{:T(128)} %bitcast.114, s32[]{:T(128)} %bitcast.115, s32[]{:T(128)} %bitcast.116, s32[]{:T(128)} %bitcast.117, s32[]{:T(128)} %bitcast.118, s32[]{:T(128)} %bitcast.119, s32[]{:T(128)} %bitcast.120, s32[]{:T(128)} %bitcast.121, s32[]{:T(128)} %bitcast.122), kind=kLoop, calls=%fused_computation.90.clone.1 | loop fusion | flops 11263 | bytes 1064 | tf_op jit(solution)/shard_map/while/body/eval_jaxpr/reduce_min | solution.py:95
  187.1 3.0 conditional.5
  191.5 6.3 %fusion.55 = (s32[]{:T(128)}, s32[256]{0:T(256)S(1)}) fusion(s32[]{:T(128)} %bitcast.114, s32[]{:T(128)} %bitcast.115, s32[]{:T(128)} %bitcast.116, s32[]{:T(128)} %bitcast.117, s32[]{:T(128)} %bitcast.118, s32[]{:T(128)} %bitcast.119, s32[]{:T(128)} %bitcast.120, s32[]{:T(128)} %bitcast.121, s32[]{:T(128)} %bitcast.122), kind=kLoop, calls=%fused_computation.90.clone.1 | loop fusion | flops 11263 | bytes 1064 | tf_op jit(solution)/shard_map/while/body/eval_jaxpr/reduce_min | solution.py:95
  200.3 6.3 %fusion.55 = (s32[]{:T(128)}, s32[256]{0:T(256)S(1)}) fusion(s32[]{:T(128)} %bitcast.114, s32[]{:T(128)} %bitcast.115, s32[]{:T(128)} %bitcast.116, s32[]{:T(128)} %bitcast.117, s32[]{:T(128)} %bitcast.118, s32[]{:T(128)} %bitcast.119, s32[]{:T(128)} %bitcast.120, s32[]{:T(128)} %bitcast.121, s32[]{:T(128)} %bitcast.122), kind=kLoop, calls=%fused_computation.90.clone.1 | loop fusion | flops 11263 | bytes 1064 | tf_op jit(solution)/shard_map/while/body/eval_jaxpr/reduce_min | solution.py:95
  207.7 3.0 conditional.5
  207.9 2.9 fusion.28
  212.1 6.3 %fusion.55 = (s32[]{:T(128)}, s32[256]{0:T(256)S(1)}) fusion(s32[]{:T(128)} %bitcast.114, s32[]{:T(128)} %bitcast.115, s32[]{:T(128)} %bitcast.116, s32[]{:T(128)} %bitcast.117, s32[]{:T(128)} %bitcast.118, s32[]{:T(128)} %bitcast.119, s32[]{:T(128)} %bitcast.120, s32[]{:T(128)} %bitcast.121, s32[]{:T(128)} %bitcast.122), kind=kLoop, calls=%fused_computation.90.clone.1 | loop fusion | flops 11263 | bytes 1064 | tf_op jit(solution)/shard_map/while/body/eval_jaxpr/reduce_min | solution.py:95
  220.9 6.3 %fusion.55 = (s32[]{:T(128)}, s32[256]{0:T(256)S(1)}) fusion(s32[]{:T(128)} %bitcast.114, s32[]{:T(128)} %bitcast.115, s32[]{:T(128)} %bitcast.116, s32[]{:T(128)} %bitcast.117, s32[]{:T(128)} %bitcast.118, s32[]{:T(128)} %bitcast.119, s32[]{:T(128)} %bitcast.120, s32[]{:T(128)} %bitcast.121, s32[]{:T(128)} %bitcast.122), kind=kLoop, calls=%fused_computation.90.clone.1 | loop fusion | flops 11263 | bytes 1064 | tf_op jit(solution)/shard_map/while/body/eval_jaxpr/reduce_min | solution.py:95
  232.5 73.5 %reduce-scatter.4.cloned.1.call-done = f32[256,2]{1,0:T(8,128)} async-done(((f32[2048,2]{1,0:T(8,128)}), f32[256,2]{1,0:T(8,128)}) %reduce-scatter.4.cloned.1.call-update) | async-done | bytes 2064
  (104 shorter events, 51.0 us)
Async XLA Ops:
  7.2 3.7 %copy-start = (s32[8]{0:T(128)S(1)}, s32[8]{0:T(128)}, u32[]{:S(2)}) copy-start(s32[8]{0:T(128)} %param.17) | copy-start | bytes 100
  7.2 27.1 %all-gather.3.cloned.1.call-start = ((), (), s32[]{:S(2)}) async-start(), calls=%async_computation.1 | async-start | bytes 1179648 | tf_op jit(solution)/shard_map/all_gather | solution.py:64
  7.9 49.9 %all-gather.5.cloned.1.call-start = ((), (), s32[]{:S(2)}) async-start(), calls=%async_computation.2 | async-start | bytes 1179648 | tf_op jit(solution)/shard_map/all_gather | solution.py:65
  8.7 297.3 %reduce-scatter.4.cloned.1.call-start = ((), (), s32[]{:S(2)}) async-start(), calls=%async_computation.3 | async-start | bytes 1179648
Sparse Core Ops, SparseCore 0:
  9.6 24.5 all-gather.2
  35.8 21.8 all-gather.4
  229.9 76.0 reduce-scatter.3
where the time goes:
time: 316 us; the launch traced here: 314 us
  waiting for transfers between devices  113 us (36%)
  other arithmetic  111 us (35%)
  local copies, waits for them, and re-layouts  33.4 us (11%)
  matrix products  22.6 us (7%)
  loops' own time  20 us (6%)
  between operations  13.9 us (4%)
    unnamed x4, waiting for transfers between devices  74.9 us
    reduce_min x8, other arithmetic, visit(): needed = jnp.min(key_pos) <= jnp.max(query_pos)  50.4 us
    reduce_min x8, other arithmetic, column_block(): needed = jnp.min(key_pos) <= jnp.max(query_pos)  50.1 us
    all_gather x1, waiting for transfers between devices, on_device(): value_piece = lax.all_gather(values, ('ctx', 'rep'), axis=0, tiled=True)  21 us
    all_gather x1, waiting for transfers between devices, on_device(): key_piece = lax.all_gather(keys, ('ctx', 'rep'), axis=0, tiled=True)  16.8 us
    gather x17, local copies, waits for them, and re-layouts, positions(): jnp.take(order_table, row_index // sub_rows) * sub_rows  11.5 us
    dynamic_slice x16, local copies, waits for them, and re-layouts, on_device(): lax.scan(advance, carried, (key_blocks, value_blocks, starts))  10.1 us
    another operation x1, loops' own time, on_device(): lax.scan(advance, carried, (key_blocks, value_blocks, starts))  9.79 us
  transfers between devices with their start and end apart: 3, of which 3 were waited for; matrix products, arithmetic and copies ran while one was open for 4% of the time, Pallas kernels for 0%

commit v1 on v0

--- a/solution.py
+++ b/solution.py
@@ -1,6 +1,11 @@
+import functools
+import math
+
 import jax
 import jax.numpy as jnp
 from jax import lax
+from jax.experimental import pallas as pl
+from jax.experimental.pallas import tpu as pltpu
 from jax.sharding import PartitionSpec as P
 
 HEAD_WIDTH = 128
@@ -122,6 +127,482 @@
     return (attended, heavy)
 
 
+CHIPS = 4
+HEADS = 8
+ROWS = 256
+PAIR = 2 * ROWS
+RATE = HEAD_WIDTH ** (-0.5) * math.log2(math.e)
+MESH = pl.DeviceIdType.MESH
+NT = (((1,), (1,)), ((), ()))
+NN = (((1,), (0,)), ((), ()))
+
+
+def fused_kernel(
+    order,
+    q_hbm,
+    k_hbm,
+    v_hbm,
+    out_hbm,
+    heavy_ref,
+    qbuf,
+    kbuf,
+    vbuf,
+    vturn,
+    expo,
+    top,
+    total,
+    tops,
+    factor,
+    sums,
+    obuf,
+    hacc,
+    hsend,
+    hrecv,
+    local_sem,
+    q_send,
+    q_recv,
+    kv_send,
+    kv_recv,
+    fwd_send,
+    h_sent,
+    h_recv,
+    o_local,
+    o_send,
+    o_recv,
+):
+    group = lax.axis_index("groups")
+    z = lax.axis_index("ctx")
+    x = lax.axis_index("head")
+    c = lax.axis_index("rep")
+    other = 1 - c
+
+    def at(zz, cc):
+        return (group, zz, x, cc)
+
+    low = 1 - z // 2
+    near = low * z + (1 - low) * (CHIPS - 1 - z)
+
+    def chip_of(step):
+        end = step
+        inner = step + 1 - 3 * (step // 3)
+        away = (1 - near) * end + near * inner
+        away = away - near * (step // 3)
+        return low * away + (1 - low) * (CHIPS - 1 - away)
+
+    wide = HEADS * HEAD_WIDTH
+    own_cols = pl.ds(pl.multiple_of(c * wide, wide), wide)
+    other_cols = pl.ds(pl.multiple_of(other * wide, wide), wide)
+    own_head = pl.ds(pl.multiple_of(c * HEAD_WIDTH, HEAD_WIDTH), HEAD_WIDTH)
+    other_head = pl.ds(pl.multiple_of(other * HEAD_WIDTH, HEAD_WIDTH), HEAD_WIDTH)
+
+    local = [
+        pltpu.make_async_copy(k_hbm.at[:, own_head], kbuf.at[z, c], local_sem.at[0]),
+        pltpu.make_async_copy(q_hbm.at[:, own_cols], qbuf.at[c], local_sem.at[1]),
+        pltpu.make_async_copy(v_hbm.at[:, own_head], vbuf.at[z, c], local_sem.at[2]),
+    ]
+    for copy in local:
+        copy.start()
+
+    barrier = pltpu.get_barrier_semaphore()
+    pl.semaphore_signal(barrier, inc=1, device_id=at(z, other), device_id_type=MESH)
+    for away in range(1, CHIPS):
+        for cc in range(2):
+            pl.semaphore_signal(
+                barrier,
+                inc=1,
+                device_id=at(lax.rem(z + away, CHIPS), cc),
+                device_id_type=MESH,
+            )
+    pl.semaphore_wait(barrier, 2 * CHIPS - 1)
+
+    def remote(src, dst, send, recv, zz, cc):
+        return pltpu.make_async_remote_copy(
+            src_ref=src,
+            dst_ref=dst,
+            send_sem=send,
+            recv_sem=recv,
+            device_id=at(zz, cc),
+            device_id_type=MESH,
+        )
+
+    pairs = ((k_hbm, kbuf), (v_hbm, vbuf))
+
+    def sibling_copy(kind):
+        src, buf = pairs[kind]
+        return remote(
+            src.at[:, other_head],
+            buf.at[z, c],
+            kv_send.at[kind, 4, 0],
+            kv_recv.at[kind, z, c],
+            z,
+            other,
+        )
+
+    def chip_copy(kind, slot, zz, cc):
+        src, buf = pairs[kind]
+        return remote(
+            src.at[:, pl.ds(cc * HEAD_WIDTH, HEAD_WIDTH)],
+            buf.at[z, c],
+            kv_send.at[kind, slot, cc],
+            kv_recv.at[kind, z, c],
+            zz,
+            cc,
+        )
+
+    def each_target(kind, act):
+        @pl.when(z < CHIPS - 1)
+        def _():
+            for cc in range(2):
+                act(chip_copy(kind, 0, z + 1, cc))
+
+        @pl.when(z > 0)
+        def _():
+            for cc in range(2):
+                act(chip_copy(kind, 1, z - 1, cc))
+
+        @pl.when(z == 0)
+        def _():
+            for cc in range(2):
+                act(chip_copy(kind, 2, z + 2, cc))
+
+        @pl.when(z == CHIPS - 1)
+        def _():
+            for cc in range(2):
+                act(chip_copy(kind, 3, z - 2, cc))
+
+    def forward_copy(kind, step, cc):
+        buf = pairs[kind][1]
+        zs = chip_of(step)
+        return remote(
+            buf.at[zs, cc],
+            buf.at[zs, cc],
+            fwd_send.at[kind, step - 1, cc],
+            kv_recv.at[kind, zs, cc],
+            (1 - low) * (CHIPS - 1),
+            c,
+        )
+
+    def wait_block(kind, zz, cc):
+        buf = pairs[kind][1]
+        remote(
+            buf.at[zz, cc],
+            buf.at[zz, cc],
+            kv_send.at[kind, 4, 1],
+            kv_recv.at[kind, zz, cc],
+            z,
+            other,
+        ).wait_recv()
+
+    q_copy = remote(q_hbm.at[:, other_cols], qbuf.at[c], q_send, q_recv, z, other)
+    k_side = sibling_copy(0)
+    v_side = sibling_copy(1)
+    each_target(0, lambda copy: copy.start())
+    k_side.start()
+    q_copy.start()
+    each_target(1, lambda copy: copy.start())
+    v_side.start()
+
+    key_row = lax.broadcasted_iota(jnp.int32, (ROWS, ROWS), 0)
+    query_lane = lax.broadcasted_iota(jnp.int32, (ROWS, ROWS), 1)
+
+    def score_piece(step, zs, hd, j, first):
+        kk = kbuf[zs].reshape(PAIR, HEAD_WIDTH)
+        cols = pl.ds(pl.multiple_of(hd * HEAD_WIDTH, HEAD_WIDTH), HEAD_WIDTH)
+        scores = lax.dot_general(kk, qbuf[j, :, cols], NT, preferred_element_type=jnp.float32)
+        halves, penalties = [], []
+        for kb in range(2):
+            half = scores[kb * ROWS : (kb + 1) * ROWS]
+            if first and kb == j:
+                half = jnp.where(key_row <= query_lane, half, NEG)
+                penalties.append(jnp.float32(0.0))
+            else:
+                penalties.append(
+                    jnp.where(order[2 * zs + kb] < order[2 * z + j], 0.0, NEG).astype(jnp.float32)
+                )
+            halves.append(half)
+        lanes = pl.ds(j * ROWS, ROWS)
+        fresh = jnp.maximum(
+            jnp.max(halves[0], axis=0, keepdims=True) + penalties[0],
+            jnp.max(halves[1], axis=0, keepdims=True) + penalties[1],
+        )
+        if not first:
+            before = top[hd, :, lanes]
+            fresh = jnp.maximum(fresh, before)
+        summed = None
+        for kb in range(2):
+            power = jnp.exp2((halves[kb] - (fresh - penalties[kb])) * RATE)
+            expo[step, hd, pl.ds(kb * ROWS, ROWS), lanes] = power.astype(jnp.bfloat16)
+            part = jnp.sum(power, axis=0, keepdims=True)
+            summed = part if summed is None else summed + part
+        if not first:
+            summed = summed + total[hd, :, lanes] * jnp.exp2((before - fresh) * RATE)
+        top[hd, :, lanes] = fresh
+        tops[step, hd, :, lanes] = fresh
+        total[hd, :, lanes] = summed
+
+    local[0].wait()
+    local[1].wait()
+    wait_block(0, z, other)
+    q_copy.wait_recv()
+
+    def own_head_scores(hd, carry):
+        for j in range(2):
+            score_piece(0, z, hd, j, True)
+        return carry
+
+    lax.fori_loop(0, HEADS, own_head_scores, 0)
+
+    inner_chip = (z == 1) | (z == 2)
+
+    def score_step(step, carry):
+        zs = chip_of(step)
+        for cc in range(2):
+            wait_block(0, zs, cc)
+
+        @pl.when(inner_chip & (step < 3))
+        def _():
+            for cc in range(2):
+                forward_copy(0, step, cc).start()
+
+        @pl.when(inner_chip & (step == 3))
+        def _():
+            for cc in range(2):
+                wait_block(1, chip_of(1), cc)
+            for cc in range(2):
+                forward_copy(1, 1, cc).start()
+
+        def head_scores(hd, inner):
+            for j in range(2):
+                score_piece(step, zs, hd, j, False)
+            return inner
+
+        lax.fori_loop(0, HEADS, head_scores, 0)
+        return carry
+
+    lax.fori_loop(1, CHIPS, score_step, 0)
+
+    @pl.when(inner_chip)
+    def _():
+        for cc in range(2):
+            wait_block(1, chip_of(2), cc)
+        for cc in range(2):
+            forward_copy(1, 2, cc).start()
+
+    def scale_step(hd, carry):
+        inverse = 1.0 / total[hd]
+        for step in range(CHIPS):
+            factor[step, hd] = jnp.exp2((tops[step, hd] - top[hd]) * RATE) * inverse
+        return carry
+
+    lax.fori_loop(0, HEADS, scale_step, 0)
+
+    def heavy_copy(step, j, zs):
+        return remote(
+            hsend.at[step, :, pl.ds(j * ROWS, ROWS)],
+            hrecv.at[z, c],
+            h_sent.at[step, j],
+            h_recv.at[z, c],
+            zs,
+            j,
+        )
+
+    def column_step(step, carry):
+        share = [factor[step, hd].astype(jnp.bfloat16) for hd in range(HEADS)]
+
+        def tile(t, inner):
+            rows = pl.ds(pl.multiple_of(t * 32, 32), 32)
+            parts = [expo[step, hd, rows, :] * share[hd] for hd in range(HEADS)]
+            while len(parts) > 1:
+                parts = [parts[i] + parts[i + 1] for i in range(0, len(parts), 2)]
+            hacc[rows, :] = parts[0]
+            return inner
+
+        lax.fori_loop(0, PAIR // 32, tile, 0)
+        ones = jnp.ones((8, PAIR), jnp.bfloat16)
+        hsend[step] = lax.dot_general(ones, hacc[...], NT, preferred_element_type=jnp.float32) * (
+            1.0 / HEADS
+        )
+        return carry
+
+    lax.fori_loop(0, CHIPS, column_step, 0)
+
+    for step in range(1, CHIPS):
+        for j in range(2):
+            heavy_copy(step, j, chip_of(step)).start()
+    for j in range(2):
+
+        @pl.when(c == j)
+        def _():
+            hrecv[z, c] = hsend[0, :, j * ROWS : (j + 1) * ROWS]
+
+        @pl.when(c != j)
+        def _():
+            heavy_copy(0, j, z).start()
+
+    local[2].wait()
+    wait_block(1, z, other)
+
+    def turn(zs):
+        vturn[...] = vbuf[zs].reshape(PAIR, HEAD_WIDTH).T
+
+    def product(step, hd):
+        return (
+            lax.dot_general(vturn[...], expo[step, hd], NN, preferred_element_type=jnp.float32)
+            * factor[step, hd]
+        )
+
+    turn(z)
+
+    def own_values(hd, carry):
+        sums[hd] = product(0, hd)
+        return carry
+
+    lax.fori_loop(0, HEADS, own_values, 0)
+
+    def wait_values(step):
+        zs = chip_of(step)
+        for cc in range(2):
+            wait_block(1, zs, cc)
+
+    def value_step(step, carry):
+        @pl.when(jnp.logical_not(inner_chip))
+        def _():
+            wait_values(step)
+
+        turn(chip_of(step))
+
+        def head_values(hd, inner):
+            sums[hd] += product(step, hd)
+            return inner
+
+        lax.fori_loop(0, HEADS, head_values, 0)
+        return carry
+
+    lax.fori_loop(1, CHIPS - 1, value_step, 0)
+    wait_values(CHIPS - 1)
+    turn(chip_of(CHIPS - 1))
+
+    def out_cols(hd):
+        return pl.ds(pl.multiple_of(c * wide + hd * HEAD_WIDTH, HEAD_WIDTH), HEAD_WIDTH)
+
+    def own_out(hd):
+        return pltpu.make_async_copy(obuf.at[c, hd], out_hbm.at[:, out_cols(hd)], o_local.at[hd])
+
+    def other_out(hd):
+        return remote(
+            obuf.at[other, hd],
+            out_hbm.at[:, out_cols(hd)],
+            o_send.at[hd],
+            o_recv.at[hd],
+            z,
+            other,
+        )
+
+    def last_values(hd, carry):
+        done = (sums[hd] + product(CHIPS - 1, hd)).astype(jnp.bfloat16)
+        for j in range(2):
+            obuf[j, hd] = done[:, j * ROWS : (j + 1) * ROWS].T
+        other_out(hd).start()
+        own_out(hd).start()
+        return carry
+
+    lax.fori_loop(0, HEADS, last_values, 0)
+
+    for zz in range(CHIPS):
+        for cc in range(2):
+
+            @pl.when((z != zz) | (c != cc))
+            def _():
+                remote(
+                    hrecv.at[zz, cc],
+                    hrecv.at[zz, cc],
+                    h_sent.at[0, 0],
+                    h_recv.at[zz, cc],
+                    z,
+                    other,
+                ).wait_recv()
+
+    for cc in range(2):
+        row = hrecv[0, cc, 0:1, :]
+        for zz in range(1, CHIPS):
+            row = row + hrecv[zz, cc, 0:1, :]
+        heavy_ref[cc : cc + 1, :] = row
+
+    for step in range(1, CHIPS):
+        for j in range(2):
+            heavy_copy(step, j, chip_of(step)).wait_send()
+    for j in range(2):
+
+        @pl.when(c != j)
+        def _():
+            heavy_copy(0, j, z).wait_send()
+
+    q_copy.wait_send()
+    for kind in range(2):
+        each_target(kind, lambda copy: copy.wait_send())
+    k_side.wait_send()
+    v_side.wait_send()
+
+    @pl.when(inner_chip)
+    def _():
+        for kind in range(2):
+            for step in range(1, 3):
+                for cc in range(2):
+                    forward_copy(kind, step, cc).wait_send()
+
+    def finish(hd, carry):
+        own_out(hd).wait()
+        other_out(hd).wait()
+        return carry
+
+    lax.fori_loop(0, HEADS, finish, 0)
+
+
+def fused_on_device(queries, keys, values, span_order):
+    width = queries.shape[1]
+    any_space = pl.BlockSpec(memory_space=pl.ANY)
+    dma = pltpu.SemaphoreType.DMA
+    return pl.pallas_call(
+        fused_kernel,
+        out_shape=(
+            jax.ShapeDtypeStruct((ROWS, width), jnp.bfloat16),
+            jax.ShapeDtypeStruct((2, ROWS), jnp.float32),
+        ),
+        in_specs=[pl.BlockSpec(memory_space=pltpu.SMEM), any_space, any_space, any_space],
+        out_specs=(any_space, pl.BlockSpec(memory_space=pltpu.VMEM)),
+        scratch_shapes=[
+            pltpu.VMEM((2, ROWS, HEADS * HEAD_WIDTH), jnp.bfloat16),
+            pltpu.VMEM((CHIPS, 2, ROWS, HEAD_WIDTH), jnp.bfloat16),
+            pltpu.VMEM((CHIPS, 2, ROWS, HEAD_WIDTH), jnp.bfloat16),
+            pltpu.VMEM((HEAD_WIDTH, PAIR), jnp.bfloat16),
+            pltpu.VMEM((CHIPS, HEADS, PAIR, PAIR), jnp.bfloat16),
+            pltpu.VMEM((HEADS, 1, PAIR), jnp.float32),
+            pltpu.VMEM((HEADS, 1, PAIR), jnp.float32),
+            pltpu.VMEM((CHIPS, HEADS, 1, PAIR), jnp.float32),
+            pltpu.VMEM((CHIPS, HEADS, 1, PAIR), jnp.float32),
+            pltpu.VMEM((HEADS, HEAD_WIDTH, PAIR), jnp.float32),
+            pltpu.VMEM((2, HEADS, ROWS, HEAD_WIDTH), jnp.bfloat16),
+            pltpu.VMEM((PAIR, PAIR), jnp.bfloat16),
+            pltpu.VMEM((CHIPS, 8, PAIR), jnp.float32),
+            pltpu.VMEM((CHIPS, 2, 8, ROWS), jnp.float32),
+            dma((3,)),
+            dma,
+            dma,
+            dma((2, 5, 2)),
+            dma((2, CHIPS, 2)),
+            dma((2, 2, 2)),
+            dma((CHIPS, 2)),
+            dma((CHIPS, 2)),
+            dma((HEADS,)),
+            dma((HEADS,)),
+            dma((HEADS,)),
+        ],
+        compiler_params=pltpu.CompilerParams(
+            collective_id=0, has_side_effects=True, vmem_limit_bytes=48 * 2**20
+        ),
+    )(span_order, queries, keys, values)
+
+
 def solution(mesh):
     placed = (
         P(("groups", "ctx", "rep"), "head"),
@@ -129,8 +610,11 @@
         P(("groups", "ctx", "rep"), "head"),
         P("groups"),
     )
+    fits = (
+        mesh.shape["ctx"] == CHIPS and mesh.shape["rep"] == 2 and mesh.shape["head"] == 2
+    )
     return jax.shard_map(
-        on_device,
+        fused_on_device if fits else on_device,
         mesh=mesh,
         in_specs=placed,
         out_specs=(P(("groups", "ctx", "rep"), "head"), P(("groups", "head"), ("ctx", "rep"))),

time: 316 us -> 44.2 us (0.14)
  waiting for transfers between devices: 113 us -> 0 us
  other arithmetic: 111 us -> 0 us
  Pallas kernels: 0 us -> 38.1 us
  local copies, waits for them, and re-layouts: 33.4 us -> 5.23 us
  matrix products: 22.6 us -> 0 us
  loops' own time: 20 us -> 0 us
  between operations: 13.9 us -> 0.65 us
    reduce_min x16 -> x0, other arithmetic: 100 us -> none  [the longest x8 50.4 us: visit(): needed = jnp.min(key_pos) <= jnp.max(query_pos)]
    unnamed x4 -> x0, waiting for transfers between devices: 74.9 us -> none
    pallas_call x0 -> x1, Pallas kernels: none -> 38.1 us  [fused_on_device(): pl.pallas_call(fused_kernel, out_shape=(jax.ShapeDtypeStruct((ROWS, width...]
    all_gather x2 -> x0, waiting for transfers between devices: 37.8 us -> none  [the longest x1 21 us: on_device(): value_piece = lax.all_gather(values, ('ctx', 'rep'), axis=0, tiled=True)]
    dot_general x9 -> x0, matrix products: 22.6 us -> none  [the longest x3 8.89 us: absorb(): jnp.einsum('hgqk,khd->hgqd', weights, value_block, preferred_element_type...]
    another operation x18 -> x0, loops' own time: 20 us -> none  [the longest x1 9.79 us: on_device(): lax.scan(advance, carried, (key_blocks, value_blocks, starts))]
    gather x17 -> x0, local copies, waits for them, and re-layouts: 11.5 us -> none  [positions(): jnp.take(order_table, row_index // sub_rows) * sub_rows]
    dynamic_slice x16 -> x0, local copies, waits for them, and re-layouts: 10.1 us -> none  [on_device(): lax.scan(advance, carried, (key_blocks, value_blocks, starts))]
  transfers between devices with their start and end apart: 3 -> 0, of which waited for: 3 -> 0; matrix products, arithmetic and copies ran while one was open for 4% -> 0% of each run, Pallas kernels for 0% -> 0%
where the time goes in v1:
time: 44.2 us; the launch traced here: 44 us
  Pallas kernels  38.1 us (86%)
  local copies, waits for them, and re-layouts  5.23 us (12%)
  between operations  0.65 us (1%)
    pallas_call x1, Pallas kernels, fused_on_device(): pl.pallas_call(fused_kernel, out_shape=(jax.ShapeDtypeStruct((ROWS, width...  38.1 us
    unnamed x10, local copies, waits for them, and re-layouts  5.23 us

profile of v1, /device:TPU:0, one launch (start us, length us, event | category | flops | bytes accessed | tf_op | source)
XLA Modules:
  0.0 44.0 jit_solution(6605234962890120085)
XLA Ops:
  0.6 0.0 copy-start
  0.6 1.2 %copy-done = bf16[256,2048]{1,0:T(8,128)(2,1)S(1)} copy-done((bf16[256,2048]{1,0:T(8,128)(2,1)S(1)}, bf16[256,2048]{1,0:T(8,128)(2,1)}, u32[]{:S(2)}) %copy-start) | copy-done | bytes 1048600
  1.9 0.0 copy-start.1
  1.9 0.9 %copy-done.1 = bf16[256,256]{1,0:T(8,128)(2,1)S(1)} copy-done((bf16[256,256]{1,0:T(8,128)(2,1)S(1)}, bf16[256,256]{1,0:T(8,128)(2,1)}, u32[]{:S(2)}) %copy-start.1) | copy-done | bytes 131096
  2.8 0.0 copy-start.2
  2.8 0.9 %copy-done.2 = bf16[256,256]{1,0:T(8,128)(2,1)S(1)} copy-done((bf16[256,256]{1,0:T(8,128)(2,1)S(1)}, bf16[256,256]{1,0:T(8,128)(2,1)}, u32[]{:S(2)}) %copy-start.2) | copy-done | bytes 131096
  3.7 0.0 copy-start.3
  3.7 0.7 %copy-done.3 = s32[8]{0:T(128)S(1)} copy-done((s32[8]{0:T(128)S(1)}, s32[8]{0:T(128)}, u32[]{:S(2)}) %copy-start.3) | copy-done | bytes 56
  4.3 38.1 %shard_map.59 = (bf16[256,2048]{1,0:T(8,128)(2,1)S(1)}, f32[2,256]{1,0:T(2,128)S(1)}) custom-call(s32[8]{0:T(128)S(1)} %copy-done.3, bf16[256,2048]{1,0:T(8,128)(2,1)S(1)} %copy-done, bf16[256,256]{1,0:T(8,128)(2,1)S(1)} %copy-done.1, bf16[256,256]{1,0:T(8,128)(2,1)S(1)} %copy-done.2), custom_call_target="tpu_custom_call" | custom-call | tf_op jit(solution)/shard_map/pallas_call | solution.py:565
  42.4 1.0 %copy.8 = bf16[256,2048]{1,0:T(8,128)(2,1)} copy(bf16[256,2048]{1,0:T(8,128)(2,1)S(1)} %get-tuple-element.4) | data formatting | bytes 2097152
  43.4 0.6 %copy.9 = f32[2,256]{1,0:T(2,128)} copy(f32[2,256]{1,0:T(2,128)S(1)} %get-tuple-element.5) | data formatting | bytes 4096
Async XLA Ops:
  0.6 1.2 %copy-start = (bf16[256,2048]{1,0:T(8,128)(2,1)S(1)}, bf16[256,2048]{1,0:T(8,128)(2,1)}, u32[]{:S(2)}) copy-start(bf16[256,2048]{1,0:T(8,128)(2,1)} %q_hbm.1) | copy-start | bytes 3145732
  1.9 0.9 %copy-start.1 = (bf16[256,256]{1,0:T(8,128)(2,1)S(1)}, bf16[256,256]{1,0:T(8,128)(2,1)}, u32[]{:S(2)}) copy-start(bf16[256,256]{1,0:T(8,128)(2,1)} %k_hbm.1) | copy-start | bytes 393220
  2.8 0.9 %copy-start.2 = (bf16[256,256]{1,0:T(8,128)(2,1)S(1)}, bf16[256,256]{1,0:T(8,128)(2,1)}, u32[]{:S(2)}) copy-start(bf16[256,256]{1,0:T(8,128)(2,1)} %v_hbm.1) | copy-start | bytes 393220
  3.7 0.7 %copy-start.3 = (s32[8]{0:T(128)S(1)}, s32[8]{0:T(128)}, u32[]{:S(2)}) copy-start(s32[8]{0:T(128)} %order.1) | copy-start | bytes 100

commit v2 on v1

--- a/solution.py
+++ b/solution.py
@@ -129,6 +129,7 @@
 
 CHIPS = 4
 HEADS = 8
+BATCH = 4
 ROWS = 256
 PAIR = 2 * ROWS
 RATE = HEAD_WIDTH ** (-0.5) * math.log2(math.e)
@@ -249,26 +250,29 @@
             cc,
         )
 
-    def each_target(kind, act):
-        @pl.when(z < CHIPS - 1)
-        def _():
-            for cc in range(2):
-                act(chip_copy(kind, 0, z + 1, cc))
-
-        @pl.when(z > 0)
-        def _():
-            for cc in range(2):
-                act(chip_copy(kind, 1, z - 1, cc))
-
-        @pl.when(z == 0)
-        def _():
-            for cc in range(2):
-                act(chip_copy(kind, 2, z + 2, cc))
-
-        @pl.when(z == CHIPS - 1)
-        def _():
-            for cc in range(2):
-                act(chip_copy(kind, 3, z - 2, cc))
+    def each_target(kind, act, outward=True, inward=True):
+        ups = (((z == 2), outward), ((z < 2), inward))
+        downs = (((z == 1), outward), ((z > 1), inward))
+        for conditions, slot, zz in ((ups, 0, z + 1), (downs, 1, z - 1)):
+            for condition, wanted in conditions:
+                if wanted:
+
+                    @pl.when(condition)
+                    def _():
+                        for cc in range(2):
+                            act(chip_copy(kind, slot, zz, cc))
+
+        if inward:
+
+            @pl.when(z == 0)
+            def _():
+                for cc in range(2):
+                    act(chip_copy(kind, 2, z + 2, cc))
+
+            @pl.when(z == CHIPS - 1)
+            def _():
+                for cc in range(2):
+                    act(chip_copy(kind, 3, z - 2, cc))
 
     def forward_copy(kind, step, cc):
         buf = pairs[kind][1]
@@ -299,94 +303,114 @@
     each_target(0, lambda copy: copy.start())
     k_side.start()
     q_copy.start()
-    each_target(1, lambda copy: copy.start())
     v_side.start()
+    each_target(1, lambda copy: copy.start(), inward=False)
 
     key_row = lax.broadcasted_iota(jnp.int32, (ROWS, ROWS), 0)
     query_lane = lax.broadcasted_iota(jnp.int32, (ROWS, ROWS), 1)
 
-    def score_piece(step, zs, hd, j, first):
+    def score_heads(step, zs, heads, first):
         kk = kbuf[zs].reshape(PAIR, HEAD_WIDTH)
-        cols = pl.ds(pl.multiple_of(hd * HEAD_WIDTH, HEAD_WIDTH), HEAD_WIDTH)
-        scores = lax.dot_general(kk, qbuf[j, :, cols], NT, preferred_element_type=jnp.float32)
-        halves, penalties = [], []
-        for kb in range(2):
-            half = scores[kb * ROWS : (kb + 1) * ROWS]
-            if first and kb == j:
-                half = jnp.where(key_row <= query_lane, half, NEG)
-                penalties.append(jnp.float32(0.0))
-            else:
-                penalties.append(
-                    jnp.where(order[2 * zs + kb] < order[2 * z + j], 0.0, NEG).astype(jnp.float32)
+        pieces = [(hd, j) for hd in heads for j in range(2)]
+        before = []
+        if not first:
+            for hd, j in pieces:
+                lanes = pl.ds(j * ROWS, ROWS)
+                before.append((top[hd, :, lanes], total[hd, :, lanes]))
+        results = []
+        for n, (hd, j) in enumerate(pieces):
+            cols = pl.ds(pl.multiple_of(hd * HEAD_WIDTH, HEAD_WIDTH), HEAD_WIDTH)
+            scores = lax.dot_general(kk, qbuf[j, :, cols], NT, preferred_element_type=jnp.float32)
+            halves, penalties = [], []
+            for kb in range(2):
+                half = scores[kb * ROWS : (kb + 1) * ROWS]
+                if first and kb == j:
+                    half = jnp.where(key_row <= query_lane, half, NEG)
+                    penalties.append(jnp.float32(0.0))
+                else:
+                    penalties.append(
+                        jnp.where(order[2 * zs + kb] < order[2 * z + j], 0.0, NEG).astype(
+                            jnp.float32
+                        )
+                    )
+                halves.append(half)
+            fresh = jnp.maximum(
+                jnp.max(halves[0], axis=0, keepdims=True) + penalties[0],
+                jnp.max(halves[1], axis=0, keepdims=True) + penalties[1],
+            )
+            if not first:
+                fresh = jnp.maximum(fresh, before[n][0])
+            summed = None
+            for kb in range(2):
+                power = jnp.exp2((halves[kb] - (fresh - penalties[kb])) * RATE)
+                expo[step, hd, pl.ds(kb * ROWS, ROWS), pl.ds(j * ROWS, ROWS)] = power.astype(
+                    jnp.bfloat16
                 )
-            halves.append(half)
-        lanes = pl.ds(j * ROWS, ROWS)
-        fresh = jnp.maximum(
-            jnp.max(halves[0], axis=0, keepdims=True) + penalties[0],
-            jnp.max(halves[1], axis=0, keepdims=True) + penalties[1],
-        )
-        if not first:
-            before = top[hd, :, lanes]
-            fresh = jnp.maximum(fresh, before)
-        summed = None
-        for kb in range(2):
-            power = jnp.exp2((halves[kb] - (fresh - penalties[kb])) * RATE)
-            expo[step, hd, pl.ds(kb * ROWS, ROWS), lanes] = power.astype(jnp.bfloat16)
-            part = jnp.sum(power, axis=0, keepdims=True)
-            summed = part if summed is None else summed + part
-        if not first:
-            summed = summed + total[hd, :, lanes] * jnp.exp2((before - fresh) * RATE)
-        top[hd, :, lanes] = fresh
-        tops[step, hd, :, lanes] = fresh
-        total[hd, :, lanes] = summed
+                part = jnp.sum(power, axis=0, keepdims=True)
+                summed = part if summed is None else summed + part
+            if not first:
+                old_top, old_total = before[n]
+                summed = summed + old_total * jnp.exp2((old_top - fresh) * RATE)
+            results.append((hd, j, fresh, summed))
+        for hd, j, fresh, summed in results:
+            lanes = pl.ds(j * ROWS, ROWS)
+            top[hd, :, lanes] = fresh
+            tops[step, hd, :, lanes] = fresh
+            total[hd, :, lanes] = summed
+
+    inner_chip = (z == 1) | (z == 2)
+
+    def pass_on(kind, step):
+        for cc in range(2):
+            wait_block(kind, chip_of(step), cc)
+        for cc in range(2):
+            forward_copy(kind, step, cc).start()
+
+    @pl.when(inner_chip)
+    def _():
+        pass_on(0, 1)
+        each_target(1, lambda copy: copy.start(), outward=False)
 
     local[0].wait()
     local[1].wait()
     wait_block(0, z, other)
     q_copy.wait_recv()
 
-    def own_head_scores(hd, carry):
-        for j in range(2):
-            score_piece(0, z, hd, j, True)
-        return carry
-
-    lax.fori_loop(0, HEADS, own_head_scores, 0)
-
-    inner_chip = (z == 1) | (z == 2)
+    def own_head_scores(t, carry):
+        score_heads(0, z, [t * BATCH + b for b in range(BATCH)], True)
+        return carry
+
+    lax.fori_loop(0, HEADS // BATCH, own_head_scores, 0)
+
+    @pl.when(jnp.logical_not(inner_chip))
+    def _():
+        each_target(1, lambda copy: copy.start(), outward=False)
+
+    def wait_keys(zs):
+        for cc in range(2):
+            wait_block(0, zs, cc)
 
     def score_step(step, carry):
         zs = chip_of(step)
-        for cc in range(2):
-            wait_block(0, zs, cc)
-
-        @pl.when(inner_chip & (step < 3))
+
+        @pl.when(jnp.logical_not(inner_chip) | (step == 3))
         def _():
-            for cc in range(2):
-                forward_copy(0, step, cc).start()
-
-        @pl.when(inner_chip & (step == 3))
-        def _():
-            for cc in range(2):
-                wait_block(1, chip_of(1), cc)
-            for cc in range(2):
-                forward_copy(1, 1, cc).start()
-
-        def head_scores(hd, inner):
-            for j in range(2):
-                score_piece(step, zs, hd, j, False)
+            wait_keys(zs)
+
+        for early, (kind, of) in enumerate(((0, 2), (1, 1), (1, 2))):
+
+            @pl.when(inner_chip & (step == early + 1))
+            def _():
+                pass_on(kind, of)
+
+        def head_scores(t, inner):
+            score_heads(step, zs, [t * BATCH + b for b in range(BATCH)], False)
             return inner
 
-        lax.fori_loop(0, HEADS, head_scores, 0)
+        lax.fori_loop(0, HEADS // BATCH, head_scores, 0)
         return carry
 
     lax.fori_loop(1, CHIPS, score_step, 0)
-
-    @pl.when(inner_chip)
-    def _():
-        for cc in range(2):
-            wait_block(1, chip_of(2), cc)
-        for cc in range(2):
-            forward_copy(1, 2, cc).start()
 
     def scale_step(hd, carry):
         inverse = 1.0 / total[hd]
@@ -394,7 +418,7 @@
             factor[step, hd] = jnp.exp2((tops[step, hd] - top[hd]) * RATE) * inverse
         return carry
 
-    lax.fori_loop(0, HEADS, scale_step, 0)
+    lax.fori_loop(0, HEADS, scale_step, 0, unroll=4)
 
     def heavy_copy(step, j, zs):
         return remote(
@@ -417,11 +441,9 @@
             hacc[rows, :] = parts[0]
             return inner
 
-        lax.fori_loop(0, PAIR // 32, tile, 0)
+        lax.fori_loop(0, PAIR // 32, tile, 0, unroll=4)
         ones = jnp.ones((8, PAIR), jnp.bfloat16)
-        hsend[step] = lax.dot_general(ones, hacc[...], NT, preferred_element_type=jnp.float32) * (
-            1.0 / HEADS
-        )
+        hsend[step] = lax.dot_general(ones, hacc[...], NT, preferred_element_type=jnp.float32)
         return carry
 
     lax.fori_loop(0, CHIPS, column_step, 0)
@@ -457,7 +479,7 @@
         sums[hd] = product(0, hd)
         return carry
 
-    lax.fori_loop(0, HEADS, own_values, 0)
+    lax.fori_loop(0, HEADS, own_values, 0, unroll=4)
 
     def wait_values(step):
         zs = chip_of(step)
@@ -475,7 +497,7 @@
             sums[hd] += product(step, hd)
             return inner
 
-        lax.fori_loop(0, HEADS, head_values, 0)
+        lax.fori_loop(0, HEADS, head_values, 0, unroll=4)
         return carry
 
     lax.fori_loop(1, CHIPS - 1, value_step, 0)
@@ -506,7 +528,7 @@
         own_out(hd).start()
         return carry
 
-    lax.fori_loop(0, HEADS, last_values, 0)
+    lax.fori_loop(0, HEADS, last_values, 0, unroll=2)
 
     for zz in range(CHIPS):
         for cc in range(2):
@@ -523,10 +545,10 @@
                 ).wait_recv()
 
     for cc in range(2):
-        row = hrecv[0, cc, 0:1, :]
+        row = hrecv[0, cc]
         for zz in range(1, CHIPS):
-            row = row + hrecv[zz, cc, 0:1, :]
-        heavy_ref[cc : cc + 1, :] = row
+            row = row + hrecv[zz, cc]
+        heavy_ref[cc] = row
 
     for step in range(1, CHIPS):
         for j in range(2):
@@ -560,13 +582,13 @@
 
 def fused_on_device(queries, keys, values, span_order):
     width = queries.shape[1]
-    any_space = pl.BlockSpec(memory_space=pl.ANY)
+    any_space = pl.BlockSpec(memory_space=pltpu.HBM)
     dma = pltpu.SemaphoreType.DMA
-    return pl.pallas_call(
+    attended, heavy = pl.pallas_call(
         fused_kernel,
         out_shape=(
             jax.ShapeDtypeStruct((ROWS, width), jnp.bfloat16),
-            jax.ShapeDtypeStruct((2, ROWS), jnp.float32),
+            jax.ShapeDtypeStruct((2, 8, ROWS), jnp.float32),
         ),
         in_specs=[pl.BlockSpec(memory_space=pltpu.SMEM), any_space, any_space, any_space],
         out_specs=(any_space, pl.BlockSpec(memory_space=pltpu.VMEM)),
@@ -598,9 +620,10 @@
             dma((HEADS,)),
         ],
         compiler_params=pltpu.CompilerParams(
-            collective_id=0, has_side_effects=True, vmem_limit_bytes=48 * 2**20
+            collective_id=0, has_side_effects=True, vmem_limit_bytes=63 * 2**20
         ),
     )(span_order, queries, keys, values)
+    return attended, heavy[:, 0, :] / HEADS
 
 
 def solution(mesh):

time: 44.2 us -> 38 us (0.86)
  Pallas kernels: 38.1 us -> 33.5 us
  local copies, waits for them, and re-layouts: 5.23 us -> 2.88 us
  other arithmetic: 0 us -> 0.72 us
    pallas_call x1, Pallas kernels: 38.1 us -> 33.5 us  [fused_on_device(): pl.pallas_call(fused_kernel, out_shape=(jax.ShapeDtypeStruct((ROWS, width...]
    unnamed x10 -> x2, local copies, waits for them, and re-layouts: 5.23 us -> 2.88 us
    div x0 -> x1, other arithmetic: none -> 0.72 us  [fused_on_device(): return (attended, heavy[:, 0, :] / HEADS)]
where the time goes in v2:
time: 38 us; the launch traced here: 37.8 us
  Pallas kernels  33.5 us (88%)
  local copies, waits for them, and re-layouts  2.88 us (8%)
  other arithmetic  0.72 us (2%)
  between operations  0.64 us (2%)
    pallas_call x1, Pallas kernels, fused_on_device(): pl.pallas_call(fused_kernel, out_shape=(jax.ShapeDtypeStruct((ROWS, width...  33.5 us
    unnamed x2, local copies, waits for them, and re-layouts  2.88 us

profile of v2, /device:TPU:0, one launch (start us, length us, event | category | flops | bytes accessed | tf_op | source)
XLA Modules:
  0.0 37.8 jit_solution(12486196799518269845)
XLA Ops:
  0.6 33.5 %shard_map.59 = (bf16[256,2048]{1,0:T(8,128)(2,1)}, f32[2,8,256]{2,1,0:T(8,128)}) custom-call(s32[8]{0:T(128)} %order.1, bf16[256,2048]{1,0:T(8,128)(2,1)} %q_hbm.1, bf16[256,256]{1,0:T(8,128)(2,1)} %k_hbm.1, bf16[256,256]{1,0:T(8,128)(2,1)} %v_hbm.1), custom_call_target="tpu_custom_call" | custom-call | tf_op jit(solution)/shard_map/pallas_call | solution.py:587
  34.2 0.7 %slice_multiply_fusion = f32[2,1,256]{2,1,0:T(1,128)S(1)} fusion(f32[2,8,256]{2,1,0:T(8,128)} %get-tuple-element.5), kind=kLoop, calls=%fused_computation.1 | loop fusion | flops 512 | bytes 4096 | tf_op jit(solution)/shard_map/div | solution.py:626
  34.9 0.6 %copy.8 = f32[2,1,256]{2,0,1:T(2,128)} copy(f32[2,1,256]{2,1,0:T(1,128)S(1)} %slice_multiply_fusion) | data formatting | bytes 4096
  35.5 2.3 %copy.10 = bf16[256,2048]{1,0:T(8,128)(2,1)} copy(bf16[256,2048]{1,0:T(8,128)(2,1)} %get-tuple-element.8) | data formatting | bytes 2097152

commit v3 on v2

--- a/solution.py
+++ b/solution.py
@@ -366,21 +366,22 @@
         for cc in range(2):
             forward_copy(kind, step, cc).start()
 
+    local[0].wait()
+    local[1].wait()
+    wait_block(0, z, other)
+    q_copy.wait_recv()
+
+    def own_head_scores(t, carry):
+        score_heads(0, z, [t * BATCH + b for b in range(BATCH)], True)
+        return carry
+
+    lax.fori_loop(0, 1, own_head_scores, 0)
     @pl.when(inner_chip)
     def _():
         pass_on(0, 1)
         each_target(1, lambda copy: copy.start(), outward=False)
 
-    local[0].wait()
-    local[1].wait()
-    wait_block(0, z, other)
-    q_copy.wait_recv()
-
-    def own_head_scores(t, carry):
-        score_heads(0, z, [t * BATCH + b for b in range(BATCH)], True)
-        return carry
-
-    lax.fori_loop(0, HEADS // BATCH, own_head_scores, 0)
+    lax.fori_loop(1, HEADS // BATCH, own_head_scores, 0)
 
     @pl.when(jnp.logical_not(inner_chip))
     def _():
@@ -418,7 +419,7 @@
             factor[step, hd] = jnp.exp2((tops[step, hd] - top[hd]) * RATE) * inverse
         return carry
 
-    lax.fori_loop(0, HEADS, scale_step, 0, unroll=4)
+    lax.fori_loop(0, HEADS, scale_step, 0, unroll=8)
 
     def heavy_copy(step, j, zs):
         return remote(
@@ -441,7 +442,7 @@
             hacc[rows, :] = parts[0]
             return inner
 
-        lax.fori_loop(0, PAIR // 32, tile, 0, unroll=4)
+        lax.fori_loop(0, PAIR // 32, tile, 0, unroll=8)
         ones = jnp.ones((8, PAIR), jnp.bfloat16)
         hsend[step] = lax.dot_general(ones, hacc[...], NT, preferred_element_type=jnp.float32)
         return carry
@@ -479,7 +480,7 @@
         sums[hd] = product(0, hd)
         return carry
 
-    lax.fori_loop(0, HEADS, own_values, 0, unroll=4)
+    lax.fori_loop(0, HEADS, own_values, 0, unroll=8)
 
     def wait_values(step):
         zs = chip_of(step)
@@ -497,7 +498,7 @@
             sums[hd] += product(step, hd)
             return inner
 
-        lax.fori_loop(0, HEADS, head_values, 0, unroll=4)
+        lax.fori_loop(0, HEADS, head_values, 0, unroll=8)
         return carry
 
     lax.fori_loop(1, CHIPS - 1, value_step, 0)
@@ -545,10 +546,10 @@
                 ).wait_recv()
 
     for cc in range(2):
-        row = hrecv[0, cc]
+        row = hrecv[0, cc, 0:1, :]
         for zz in range(1, CHIPS):
-            row = row + hrecv[zz, cc]
-        heavy_ref[cc] = row
+            row = row + hrecv[zz, cc, 0:1, :]
+        heavy_ref[cc : cc + 1, :] = row / HEADS
 
     for step in range(1, CHIPS):
         for j in range(2):
@@ -588,7 +589,7 @@
         fused_kernel,
         out_shape=(
             jax.ShapeDtypeStruct((ROWS, width), jnp.bfloat16),
-            jax.ShapeDtypeStruct((2, 8, ROWS), jnp.float32),
+            jax.ShapeDtypeStruct((2, ROWS), jnp.float32),
         ),
         in_specs=[pl.BlockSpec(memory_space=pltpu.SMEM), any_space, any_space, any_space],
         out_specs=(any_space, pl.BlockSpec(memory_space=pltpu.VMEM)),
@@ -623,7 +624,7 @@
             collective_id=0, has_side_effects=True, vmem_limit_bytes=63 * 2**20
         ),
     )(span_order, queries, keys, values)
-    return attended, heavy[:, 0, :] / HEADS
+    return attended, heavy
 
 
 def solution(mesh):

time: 38 us -> 36.3 us (0.955)
  Pallas kernels: 33.5 us -> 32.6 us
  other arithmetic: 0.72 us -> 0 us
    pallas_call x1, Pallas kernels: 33.5 us -> 32.6 us  [fused_on_device(): pl.pallas_call(fused_kernel, out_shape=(jax.ShapeDtypeStruct((ROWS, width...]
    div x1 -> x0, other arithmetic: 0.72 us -> none  [fused_on_device(): return (attended, heavy[:, 0, :] / HEADS)]
    unnamed x2 -> x4, local copies, waits for them, and re-layouts: 2.88 us -> 2.89 us
where the time goes in v3:
time: 36.3 us; the launch traced here: 36.1 us
  Pallas kernels  32.6 us (90%)
  local copies, waits for them, and re-layouts  2.89 us (8%)
  between operations  0.65 us (2%)
    pallas_call x1, Pallas kernels, fused_on_device(): pl.pallas_call(fused_kernel, out_shape=(jax.ShapeDtypeStruct((ROWS, width...  32.6 us
    unnamed x4, local copies, waits for them, and re-layouts  2.89 us

profile of v3, /device:TPU:0, one launch (start us, length us, event | category | flops | bytes accessed | tf_op | source)
XLA Modules:
  0.0 36.1 jit_solution(1617519895445413809)
XLA Ops:
  0.6 32.6 %shard_map.59 = (bf16[256,2048]{1,0:T(8,128)(2,1)}, f32[2,256]{1,0:T(2,128)}) custom-call(s32[8]{0:T(128)} %order.1, bf16[256,2048]{1,0:T(8,128)(2,1)} %q_hbm.1, bf16[256,256]{1,0:T(8,128)(2,1)} %k_hbm.1, bf16[256,256]{1,0:T(8,128)(2,1)} %v_hbm.1), custom_call_target="tpu_custom_call" | custom-call | tf_op jit(solution)/shard_map/pallas_call | solution.py:588
  33.2 0.0 copy-start
  33.3 2.3 %copy.8 = bf16[256,2048]{1,0:T(8,128)(2,1)} copy(bf16[256,2048]{1,0:T(8,128)(2,1)} %get-tuple-element.4) | data formatting | bytes 2097152
  35.6 0.0 copy-done
  35.6 0.6 %copy.9 = f32[2,256]{1,0:T(2,128)} copy(f32[2,256]{1,0:T(2,128)S(1)} %copy-done) | data formatting | bytes 4096
Async XLA Ops:
  33.2 2.3 %copy-start = (f32[2,256]{1,0:T(2,128)S(1)}, f32[2,256]{1,0:T(2,128)}, u32[]{:S(2)}) copy-start(f32[2,256]{1,0:T(2,128)} %get-tuple-element.5) | copy-start | bytes 6148
